TPU v7x, 32 devices: a whole 2x2x4 slice. The times are simulated.
32 devices in a mesh: groups: 2 (over y), dp: 4 (over z), fsdp: 4 (over x, core).
Axes of the slice: x: 2, y: 2, z: 4, core: 2. Of those that a mesh axis runs over, the one named last changes fastest.
Arguments:
- tokens: bfloat16 [8192, 5120], P(('groups', 'dp', 'fsdp')), parts along dimension 0, may hold values from -6 to 6
- row_tenant_index: int32 [8192, 1], P(('groups', 'dp', 'fsdp')), parts along dimension 0, may hold values from 0 to 31; in each aligned block of 256 rows (0 to 255, 256 to 511, ...) at most 8 rows name the same one
- tenant_adapter_slot: int32 [32], replicated, may hold values from 0 to 31, each once
- live_row_counts: int32 [32], P(('groups', 'dp', 'fsdp')), parts along dimension 0, may hold values from 192 to 256
- readout: bfloat16 [8192, 1024], P(('groups', 'dp', 'fsdp')), parts along dimension 0, may hold values from -0.125 to 0.125
- advantage: bfloat16 [8192], P(('groups', 'dp', 'fsdp')), parts along dimension 0, may hold values from -6 to 6
- base_value_matrix: bfloat16 [5120, 1024], P('fsdp'), may hold values from -0.078125 to 0.078125
- adapter_down_maps: bfloat16 [32, 5120, 32], P('dp'), may hold values from -0.078125 to 0.078125
- adapter_up_maps: bfloat16 [32, 32, 1024], P('dp'), may hold values from -0.5 to 0.5
Outputs:
- values: bfloat16 [8192, 1024], P(('groups', 'dp', 'fsdp')), parts along dimension 0
- kl_rows: float32 [8192], P(('groups', 'dp', 'fsdp')), parts along dimension 0
- down_map_gradient: float32 [64, 5120, 32], P(('groups', 'dp'), 'fsdp'), parts along dimension 0
- up_map_gradient: float32 [64, 32, 1024], P(('groups', 'dp'), None, 'fsdp'), parts along dimension 0
There are 2 independent parts, one for each index of `groups`. A program takes and returns all parts, laid end to end along the dimension named above; an argument that names none is the same for every part. Nothing has to cross between parts.
Inputs may be any that keep to these rules, and one draw needn't show every extreme that they name: `row_tenant_index`: within the rows of one device no tenant is named more than 8 times.
All inputs are finite; a program needn't handle non-finite values.
Results may differ from a plain program's by a relative error of at most 0.008.
Values may be sent and summed in bfloat16 or wider, within the bound.
A program may use at most 128 MiB of HBM per device.

v0:
```python
import jax
import jax.numpy as jnp
from jax import lax
from jax.sharding import PartitionSpec as P

TEN_DEV = 8
MOST = 8


adapter_scale = 2.0
kl_weight = 0.5


def slot_lookup_table(flattened_tenant, local):
    return (flattened_tenant[:, None] - 1 == jnp.arange(local, dtype=jnp.int32)[None, :]).astype(
        jnp.float32
    )


def adapter_value_forward(flattened_input, flattened_tenant, adapter_down_maps, adapter_up_maps):
    slot_indicator = slot_lookup_table(flattened_tenant, adapter_down_maps.shape[0])
    every_owner = jnp.einsum(
        "au,wuq->awq", flattened_input, adapter_down_maps, preferred_element_type=jnp.float32
    )
    low = jnp.sum(slot_indicator[:, :, None] * every_owner, axis=1).astype(jnp.bfloat16)
    rank_space_widened = (slot_indicator[:, :, None] * low.astype(jnp.float32)[:, None, :]).astype(
        jnp.bfloat16
    )
    adapter_difference = (
        adapter_scale
        * jnp.einsum(
            "kqv,qvy->ky", rank_space_widened, adapter_up_maps, preferred_element_type=jnp.float32
        )
    ).astype(jnp.bfloat16)
    return (slot_indicator, rank_space_widened, adapter_difference)


def kl_terms(delta32, direction, adv, live):
    dir32 = direction.astype(jnp.float32)
    gap = jnp.sum(delta32 * dir32, axis=1)
    kl = jnp.where(live, jnp.exp(-gap) + gap - 1.0, 0.0)
    coeff = jnp.where(live, kl_weight * (1.0 - jnp.exp(-gap)) - adv.astype(jnp.float32), 0.0)
    output_gradient = (coeff[:, None] * dir32).astype(jnp.bfloat16)
    return (kl, output_gradient)


def adapter_gradients(
    flattened_input, slot_indicator, rank_space_widened, output_gradient, adapter_up_maps
):
    backward_everything = jnp.einsum(
        "qi,yli->qyl", output_gradient, adapter_up_maps, preferred_element_type=jnp.float32
    )
    rank_space_gradient = (
        adapter_scale * jnp.sum(slot_indicator[:, :, None] * backward_everything, axis=1)
    ).astype(jnp.bfloat16)
    grad_wide = (
        slot_indicator[:, :, None] * rank_space_gradient.astype(jnp.float32)[:, None, :]
    ).astype(jnp.bfloat16)
    down_map_gradient = jnp.einsum(
        "md,mtr->tdr", flattened_input, grad_wide, preferred_element_type=jnp.float32
    )
    up_map_gradient = adapter_scale * jnp.einsum(
        "mtr,me->tre", rank_space_widened, output_gradient, preferred_element_type=jnp.float32
    )
    return (down_map_gradient, up_map_gradient)


def per_device(
    tokens,
    row_tenant_index,
    tenant_adapter_slot,
    live_row_counts,
    readout,
    advantage,
    base_value_matrix,
    adapter_down_maps,
    adapter_up_maps,
):
    rows, width = tokens.shape
    proj = base_value_matrix.shape[1]
    owners = lax.axis_size("dp")
    per_owner = TEN_DEV * MOST
    buffer_rows = owners * per_owner
    live = jnp.arange(rows, dtype=jnp.int32) < live_row_counts[0]
    count_ten = tenant_adapter_slot.shape[0]
    match = row_tenant_index[:, 0][:, None] == jnp.arange(count_ten, dtype=jnp.int32)[None, :]
    adapter_slot_index = jnp.sum(jnp.where(match, tenant_adapter_slot[None, :], 0), axis=1)
    owner = adapter_slot_index // TEN_DEV
    within = adapter_slot_index % TEN_DEV
    owner_hot = (
        (owner[:, None] == jnp.arange(owners, dtype=jnp.int32)[None, :]) & live[:, None]
    ).astype(jnp.int32)
    rank = jnp.sum((jnp.cumsum(owner_hot, axis=0) - owner_hot) * owner_hot, axis=1)
    target = jnp.where(live, owner * per_owner + rank, buffer_rows)
    source_row = (
        jnp.full((buffer_rows + 1,), rows, jnp.int32)
        .at[target]
        .set(jnp.arange(rows, dtype=jnp.int32))[:buffer_rows]
    )
    tag_pad = jnp.concatenate([jnp.where(live, within + 1, 0), jnp.zeros((1,), jnp.int32)])
    send_tag = tag_pad[source_row].reshape(owners, per_owner)
    x_pad = jnp.concatenate([tokens, jnp.zeros((1, width), tokens.dtype)], axis=0)
    base = jnp.dot(
        tokens,
        lax.all_gather(base_value_matrix, "fsdp", axis=0, tiled=True),
        preferred_element_type=jnp.float32,
    )
    send_x = x_pad[source_row].reshape(owners, per_owner, width)
    recv_x, recv_tag = (
        lax.all_to_all(send_x, "dp", split_axis=0, concat_axis=0, tiled=True),
        lax.all_to_all(send_tag, "dp", split_axis=0, concat_axis=0, tiled=True),
    )
    flattened_input = recv_x.reshape(buffer_rows, width)
    flattened_tenant = recv_tag.reshape(buffer_rows)
    slot_indicator, rank_space_widened, adapter_difference = adapter_value_forward(
        flattened_input, flattened_tenant, adapter_down_maps, adapter_up_maps
    )
    back = lax.all_to_all(
        adapter_difference.reshape(owners, per_owner, proj),
        "dp",
        split_axis=0,
        concat_axis=0,
        tiled=True,
    ).reshape(buffer_rows, proj)
    picked = back[jnp.minimum(target, buffer_rows - 1)]
    delta_rows = jnp.where(live[:, None], picked.astype(jnp.float32), 0.0)
    kl_rows, output_gradient = kl_terms(delta_rows, readout, advantage, live)
    cot_pad = jnp.concatenate(
        [output_gradient, jnp.zeros((1, proj), output_gradient.dtype)], axis=0
    )
    send_cot = cot_pad[source_row].reshape(owners, per_owner, proj)
    owner_output_gradient = lax.all_to_all(
        send_cot, "dp", split_axis=0, concat_axis=0, tiled=True
    ).reshape(buffer_rows, proj)
    down_map_gradient, up_map_gradient = adapter_gradients(
        flattened_input, slot_indicator, rank_space_widened, owner_output_gradient, adapter_up_maps
    )
    out_a, out_b = (
        lax.psum_scatter(down_map_gradient, "fsdp", scatter_dimension=1, tiled=True),
        lax.psum_scatter(up_map_gradient, "fsdp", scatter_dimension=2, tiled=True),
    )
    values = (base + delta_rows).astype(jnp.bfloat16)
    return (values, kl_rows, out_a, out_b)


def solution(mesh):
    placed = (
        P(("groups", "dp", "fsdp"), None),
        P(("groups", "dp", "fsdp"), None),
        P(),
        P(("groups", "dp", "fsdp")),
        P(("groups", "dp", "fsdp"), None),
        P(("groups", "dp", "fsdp")),
        P("fsdp", None),
        P("dp", None, None),
        P("dp", None, None),
    )
    return jax.shard_map(
        per_device,
        mesh=mesh,
        in_specs=placed,
        out_specs=(
            P(("groups", "dp", "fsdp"), None),
            P(("groups", "dp", "fsdp")),
            P(("groups", "dp"), "fsdp", None),
            P(("groups", "dp"), None, "fsdp"),
        ),
        check_vma=False,
    )
```

profile of v0, /device:TPU:0, one launch (start us, length us, event | category | flops | bytes accessed | tf_op | source)
XLA Modules:
  0.0 230.7 jit_solution(5047456676080031226)
XLA Ops:
  8.8 1.2 reduce-window.6
  10.5 1.4 scatter_custom_fusion
  11.9 1.9 gather_fusion
  14.5 6.3 %all-to-all-start = ((s32[4,1,64]{2,1,0:T(1,128)}), s32[4,1,64]{2,1,0:T(1,128)S(1)}, u32[]{:S(2)}, u32[]{:S(2)}) async-start(s32[4,1,64]{2,1,0:T(1,128)} %all_to_all.15), calls=%async_computation | async-start | bytes 4096 | tf_op jit(solution)/shard_map/all_to_all | solution.py:111
  20.9 4.3 %concatenate.10 = bf16[257,5120]{1,0:T(8,128)(2,1)} pad(bf16[256,5120]{1,0:T(8,128)(2,1)} %param.9, bf16[]{:T(256)} %constant.59.clone.1), padding=0_1x0_0 | pad | bytes 5253122 | tf_op jit(solution)/shard_map/concatenate | solution.py:102
  25.2 8.7 %gather_fusion.1 = bf16[256,5120]{1,0:T(8,128)(2,1)} fusion(bf16[257,5120]{1,0:T(8,128)(2,1)} %concatenate.10, s32[1024]{0:T(1024)S(1)} %pad_clamp_fusion.1), kind=kCustom, calls=%fused_computation.1 | custom fusion | bytes 5243904 | tf_op jit(solution)/shard_map/gather | solution.py:108
  33.9 5.0 %all-to-all-start.1 = ((bf16[4,64,5120]{2,1,0:T(8,128)(2,1)}), bf16[4,64,5120]{2,1,0:T(8,128)(2,1)}, u32[]{:S(2)}, u32[]{:S(2)}) async-start(bf16[4,64,5120]{2,1,0:T(8,128)(2,1)} %bitcast.71), calls=%async_computation.1 | async-start | bytes 5242880 | tf_op jit(solution)/shard_map/all_to_all | solution.py:110
  39.0 59.1 %all-to-all-done.1 = bf16[4,64,5120]{2,1,0:T(8,128)(2,1)} async-done(((bf16[4,64,5120]{2,1,0:T(8,128)(2,1)}), bf16[4,64,5120]{2,1,0:T(8,128)(2,1)}, u32[]{:S(2)}, u32[]{:S(2)}) %all-to-all-start.1) | async-done | bytes 2621472 | tf_op jit(solution)/shard_map/all_to_all | solution.py:110
  98.1 2.7 %fusion.22 = f32[256,256]{0,1:S(1)} fusion(bf16[256,5120]{1,0:T(8,128)(2,1)} %bitcast.9, bf16[5120,256]{0,1:T(8,128)(2,1)S(1)} %bitcast.69), kind=kOutput, calls=%fused_computation.76 | convolution fusion | flops 671088640 | bytes 5505024
  100.8 1.1 fusion.2
  101.9 3.5 %all-to-all-start.2 = ((bf16[4,64,1024]{2,1,0:T(8,128)(2,1)}), bf16[4,64,1024]{2,1,0:T(8,128)(2,1)S(1)}, u32[]{:S(2)}, u32[]{:S(2)}) async-start(bf16[4,64,1024]{2,1,0:T(8,128)(2,1)} %bitcast.75), calls=%async_computation.2 | async-start | bytes 1048576 | tf_op jit(solution)/shard_map/all_to_all | solution.py:118
  105.5 13.9 %all-to-all-done.2 = bf16[4,64,1024]{2,1,0:T(8,128)(2,1)S(1)} async-done(((bf16[4,64,1024]{2,1,0:T(8,128)(2,1)}), bf16[4,64,1024]{2,1,0:T(8,128)(2,1)S(1)}, u32[]{:S(2)}, u32[]{:S(2)}) %all-to-all-start.2) | async-done | bytes 524320 | tf_op jit(solution)/shard_map/all_to_all | solution.py:118
  119.4 2.0 gather_fusion.2
  121.3 1.5 fusion.4
  123.4 1.2 fusion.5
  124.7 2.0 gather_fusion.3
  126.6 17.4 %all_to_all.24 = bf16[4,64,1024]{2,1,0:T(8,128)(2,1)S(1)} all-to-all(bf16[4,64,1024]{2,1,0:T(8,128)(2,1)} %bitcast.74), channel_id=1, replica_groups=mesh['groups'=2,'dp'=4,'fsdp'=4] {'dp'}, dimensions={0} | all-to-all | bytes 1048576 | tf_op jit(solution)/shard_map/all_to_all | solution.py:132
  144.0 1.3 convolution_multiply_fusion
  145.6 1.4 fusion.3
  147.0 5.0 %convolution_bitcast_fusion = f32[8,5120,32]{1,2,0:T(8,128)} fusion(bf16[256,5120,1]{1,0,2:T(8,128)(2,1)} %bitcast.20, f32[256,32]{0,1:T(8,128)S(1)} %fusion.12, f32[256,8]{0,1:T(8,128)S(1)} %fusion.13), kind=kOutput, calls=%fused_computation.5 | convolution fusion | flops 671219712 | bytes 7905280 | tf_op jit(solution)/shard_map/md,mtr->tdr/dot_general | solution.py:59
  152.0 1.0 copy-done.1
  153.0 8.5 %fusion.1 = bf16[256,1024]{1,0:T(8,128)(2,1)} fusion(bf16[256,5120]{1,0:T(8,128)(2,1)} %param.9, bf16[5120,1024]{1,0:T(8,128)(2,1)} %all-gather.2.cloned.1.call-done, bf16[256,1024]{1,0:T(8,128)(2,1)S(1)} %copy-done.1, pred[256]{0:T(512)(128)(4,1)S(1)} %iota_compare_fusion.3), kind=kOutput, calls=%fused_computation.12 | convolution fusion | flops 2685403136 | bytes 14156032 | tf_op jit(solution)/shard_map/dot_general | solution.py:103
  161.5 8.0 %reduce-scatter.5.cloned.1.call-done = f32[8,32,256]{2,1,0:T(8,128)} async-done(((f32[8,32,1024]{2,1,0:T(8,128)}), f32[8,32,256]{2,1,0:T(8,128)}) %reduce-scatter.5.cloned.1.call-update) | async-done | bytes 262160 | tf_op jit(solution)/shard_map/reduce_scatter | solution.py:140
  169.5 54.7 %reduce-scatter.3.cloned.1.call-done = f32[8,1280,32]{1,2,0:T(8,128)} async-done(((f32[8,5120,32]{1,2,0:T(8,128)}), f32[8,1280,32]{1,2,0:T(8,128)}) %reduce-scatter.3.cloned.1.call-update) | async-done | bytes 1310736 | tf_op jit(solution)/shard_map/reduce_scatter | solution.py:139
  (48 shorter events, 3.1 us)
Async XLA Ops:
  7.2 90.9 %copy-start = (bf16[8,5120,32]{1,2,0:T(8,128)(2,1)S(1)}, bf16[8,5120,32]{1,2,0:T(8,128)(2,1)}, u32[]{:S(2)}) copy-start(bf16[8,5120,32]{1,2,0:T(8,128)(2,1)} %param.16) | copy-start | bytes 7864324
  7.2 1.5 copy-start.2
  7.2 1.5 copy-start.3
  7.2 144.8 %all-gather.2.cloned.1.call-start = ((), (), s32[]{:S(2)}) async-start(), calls=%async_computation.6 | async-start | bytes 13107200 | tf_op jit(solution)/shard_map/all_gather | solution.py:105
  14.5 19.3 %all-to-all-start = ((s32[4,1,64]{2,1,0:T(1,128)}), s32[4,1,64]{2,1,0:T(1,128)S(1)}, u32[]{:S(2)}, u32[]{:S(2)}) async-start(s32[4,1,64]{2,1,0:T(1,128)} %all_to_all.15), calls=%async_computation | async-start | bytes 4096 | tf_op jit(solution)/shard_map/all_to_all | solution.py:111
  33.9 64.2 %all-to-all-start.1 = ((bf16[4,64,5120]{2,1,0:T(8,128)(2,1)}), bf16[4,64,5120]{2,1,0:T(8,128)(2,1)}, u32[]{:S(2)}, u32[]{:S(2)}) async-start(bf16[4,64,5120]{2,1,0:T(8,128)(2,1)} %bitcast.71), calls=%async_computation.1 | async-start | bytes 5242880 | tf_op jit(solution)/shard_map/all_to_all | solution.py:110
  98.1 2.7 %copy-start.5 = (bf16[8,32,1024]{2,1,0:T(8,128)(2,1)S(1)}, bf16[8,32,1024]{2,1,0:T(8,128)(2,1)}, u32[]{:S(2)}) copy-start(bf16[8,32,1024]{2,1,0:T(8,128)(2,1)} %param.17) | copy-start | bytes 1572868
  101.9 17.4 %all-to-all-start.2 = ((bf16[4,64,1024]{2,1,0:T(8,128)(2,1)}), bf16[4,64,1024]{2,1,0:T(8,128)(2,1)S(1)}, u32[]{:S(2)}, u32[]{:S(2)}) async-start(bf16[4,64,1024]{2,1,0:T(8,128)(2,1)} %bitcast.75), calls=%async_computation.2 | async-start | bytes 1048576 | tf_op jit(solution)/shard_map/all_to_all | solution.py:118
  105.4 64.1 %reduce-scatter.5.cloned.1.call-start = ((), (), s32[]{:S(2)}) async-start(), calls=%async_computation.8 | async-start | bytes 1310720 | tf_op jit(solution)/shard_map/reduce_scatter | solution.py:140
  119.4 3.5 %copy-start.4 = (bf16[256]{0:T(256)(128)(2,1)S(1)}, bf16[256]{0:T(256)(128)(2,1)}, u32[]{:S(2)}) copy-start(bf16[256]{0:T(256)(128)(2,1)} %param.14) | copy-start | bytes 1540
  145.3 78.8 %reduce-scatter.3.cloned.1.call-start = ((), (), s32[]{:S(2)}) async-start(), calls=%async_computation.7 | async-start | bytes 6553600 | tf_op jit(solution)/shard_map/reduce_scatter | solution.py:139
  151.9 1.1 copy-start.1
Sparse Core Ops, SparseCore 0:
  9.6 72.8 all-gather.1
  145.5 23.9 reduce-scatter.4
  172.8 51.3 reduce-scatter.2
where the time goes:
time: 231 us
  waiting for transfers between devices  136 us (59%)
  local copies, waits for them, and re-layouts  22.4 us (10%)
  matrix products  19.9 us (9%)
  blocking collectives  17.4 us (8%)
  starting transfers between devices  15.1 us (7%)
  between operations  14.7 us (6%)
  other arithmetic  4.9 us (2%)
    all_to_all x1, waiting for transfers between devices, per_device(): lax.all_to_all(send_x, 'dp', split_axis=0, concat_axis=0, tiled=True)  59.1 us
    reduce_scatter x1, waiting for transfers between devices, per_device(): lax.psum_scatter(down_map_gradient, 'fsdp', scatter_dimension=1, tiled=True)  54.7 us
    all_to_all x1, blocking collectives, per_device(): lax.all_to_all(send_cot, 'dp', split_axis=0, concat_axis=0, tiled=True)  17.4 us
    all_to_all x1, waiting for transfers between devices, per_device(): lax.all_to_all(adapter_difference.reshape(owners, per_owner, proj), 'dp',...  13.9 us
    gather x1, local copies, waits for them, and re-layouts, per_device(): send_x = x_pad[source_row].reshape(owners, per_owner, width)  8.69 us
    dot_general x1, matrix products, per_device(): jnp.dot(tokens, lax.all_gather(base_value_matrix, 'fsdp', axis=0, tiled=T...  8.47 us
    reduce_scatter x1, waiting for transfers between devices, per_device(): lax.psum_scatter(up_map_gradient, 'fsdp', scatter_dimension=2, tiled=True)  8.02 us
    all_to_all x1, starting transfers between devices, per_device(): lax.all_to_all(send_tag, 'dp', split_axis=0, concat_axis=0, tiled=True)  6.32 us
  transfers between devices with their start and end apart: 6, of which 4 were waited for; matrix products, arithmetic and copies ran while one was open for 20% of the time, Pallas kernels for 0%

commit v1 on v0

v1 whole, which is shorter than its diff:
```python
import functools

import jax
import jax.numpy as jnp
from jax import lax
from jax.experimental import pallas as pl
from jax.experimental.pallas import tpu as pltpu
from jax.sharding import PartitionSpec as P

MOST = 8

adapter_scale = 2.0
kl_weight = 0.5
bf16 = jnp.bfloat16
f32 = jnp.float32
LANES = 128


def rounded(a):
    return lax.reduce_precision(a.astype(f32), 8, 7).astype(bf16)


def nt(a, b):
    return lax.dot_general(a, b, (((1,), (1,)), ((), ())), preferred_element_type=f32)


def tn(a, b):
    return lax.dot_general(a, b, (((0,), (0,)), ((), ())), preferred_element_type=f32)


def adapters_kernel(
    owners, shares, rank,
    pick_ref, tokens_ref, readout_ref, adv_ref, down_ref, up_ref,
    delta_ref, kl_ref, down_grad_ref, up_grad_ref,
    x_send, x_recv, low_send, low_recv, up_all, m_send, m_recv, dirs,
    xs, xr, ls, lr, ms, mr, us, ur, vs, vr,
):
    peers = owners * shares
    d, f = lax.axis_index("dp"), lax.axis_index("fsdp")
    me = d * shares + f
    buffer_rows, rows = pick_ref.shape
    block = buffer_rows // owners
    wide = up_ref.shape[0]
    part = tokens_ref.shape[1] // shares
    cut = readout_ref.shape[1] // shares

    def where_is(p):
        return {"dp": p // shares, "fsdp": lax.rem(p, shares)}

    def copy(src, dst, send, recv, p):
        return pltpu.make_async_remote_copy(
            src_ref=src, dst_ref=dst, send_sem=send, recv_sem=recv,
            device_id=where_is(p), device_id_type=pl.DeviceIdType.MESH,
        )

    def x_copy(to, source):
        return copy(x_send.at[to], x_recv.at[source], xs.at[to], xr.at[source], to)

    def low_copy(to, source):
        return copy(low_send.at[to], low_recv.at[source], ls.at[to], lr.at[source], to)

    def m_copy(to, source):
        return copy(m_send.at[to], m_recv.at[source], ms.at[to], mr.at[source], to)

    def other(k):
        return lax.rem(me + k, peers)

    barrier = pltpu.get_barrier_semaphore()
    for k in range(1, peers):
        pl.semaphore_signal(
            barrier, inc=1, device_id=where_is(other(k)), device_id_type=pl.DeviceIdType.MESH
        )
    pl.semaphore_wait(barrier, peers - 1)

    my_cut = pl.ds(pl.multiple_of(f * cut, LANES), cut)

    def up_copy(to_d, source):
        return copy(up_ref.at[:, my_cut], up_all.at[f, source], us.at[to_d], ur.at[source], to_d * shares + f)

    for j in range(1, owners):
        up_copy(lax.rem(d + j, owners), d).start()
    up_all[f, d] = up_ref[:, my_cut]

    for i in range(shares):
        s = lax.rem(f + i, shares)
        columns = pl.ds(pl.multiple_of(s * part, LANES), part)
        moved = jnp.dot(pick_ref[...], tokens_ref[:, columns], preferred_element_type=f32).astype(bf16)
        for o in range(owners):
            x_send[o * shares + s] = moved[o * block : (o + 1) * block]
        for j in range(owners):
            o = lax.rem(d + owners // 2 + j, owners)
            if i == 0 and j == owners - owners // 2:
                continue
            x_copy(o * shares + s, me).start()
    x_recv[me] = x_send[me]

    def up_on(to_f, source):
        return copy(up_all.at[f], up_all.at[source], vs.at[to_f], vr.at[source], d * shares + to_f)

    for j in range(1, owners):
        up_copy(d, lax.rem(d + j, owners)).wait_recv()
    for j in range(1, shares):
        s = lax.rem(f + j, shares)
        copy(up_all.at[f], up_all.at[f], vs.at[s], vr.at[f], d * shares + s).start()

    dirs[...] = jnp.dot(pick_ref[...], readout_ref[...], preferred_element_type=f32)
    hit = pick_ref[...].astype(f32) > 0.5
    adv = jnp.sum(jnp.where(hit, adv_ref[...], 0.0), axis=1, keepdims=True)

    my_part = pl.ds(pl.multiple_of(f * part, LANES), part)
    own = (
        lax.broadcasted_iota(jnp.int32, (block, wide), 0) // MOST
        == lax.broadcasted_iota(jnp.int32, (block, wide), 1) // rank
    )

    def low_of(q):
        every = jnp.where(own, nt(x_recv[q], down_ref[:, my_part]), 0.0)
        total = every[:, :LANES]
        for g in range(1, wide // LANES):
            total = total + every[:, g * LANES : (g + 1) * LANES]
        return total

    low_recv[me] = low_of(me)

    def step(k, carry):
        q = lax.rem(me + k, peers)
        x_copy(q, q).wait_recv()
        low_send[q] = low_of(q)
        low_copy(q, me).start()
        return carry

    lax.fori_loop(1, peers, step, 0)

    for j in range(1, shares):
        up_on(f, lax.rem(f + j, shares)).wait_recv()

    for k in range(1, peers):
        low_copy(other(k), other(k)).wait_recv()
    blocks = []
    for o in range(owners):
        total = low_recv[o * shares]
        for s in range(1, shares):
            total = total + low_recv[o * shares + s]
        blocks.append(total)
    low = jnp.concatenate(blocks, axis=0).astype(bf16)
    low32 = low.astype(f32)
    columns = owners * wide
    mine = (
        lax.broadcasted_iota(jnp.int32, (buffer_rows, columns), 0) // MOST
        == lax.broadcasted_iota(jnp.int32, (buffer_rows, columns), 1) // rank
    )
    spread = jnp.where(mine, jnp.concatenate([low32] * (columns // LANES), axis=1), 0.0).astype(bf16)
    deltas = []
    gap = jnp.zeros((buffer_rows, 1), f32)
    for s in range(shares):
        up = up_all[s].reshape(columns, cut)
        delta = (adapter_scale * jnp.dot(spread, up, preferred_element_type=f32)).astype(bf16)
        deltas.append(delta)
        gap = gap + jnp.sum(delta.astype(f32) * dirs[:, s * cut : (s + 1) * cut], axis=1, keepdims=True)
    small = jnp.exp(-gap)
    coeff = kl_weight * (1.0 - small) - adv
    back = jnp.zeros((buffer_rows, columns), f32)
    for s in range(shares):
        cot = (coeff * dirs[:, s * cut : (s + 1) * cut]).astype(bf16)
        for o in range(owners):
            m_send[o * shares + s, :, LANES:] = cot[o * block : (o + 1) * block]
        back = back + nt(cot, up_all[s].reshape(columns, cut))
    back = jnp.where(mine, back, 0.0)
    total = back[:, :LANES]
    for g in range(1, columns // LANES):
        total = total + back[:, g * LANES : (g + 1) * LANES]
    packed = (adapter_scale * total + pltpu.roll(low32, LANES // 2, 1)).astype(bf16)
    for o in range(owners):
        for s in range(shares):
            m_send[o * shares + s, :, :LANES] = packed[o * block : (o + 1) * block]
    for k in range(1, peers):
        m_copy(other(k), me).start()
    m_recv[me] = m_send[me]

    kl_ref[...] = jnp.sum(jnp.where(hit, small + gap - 1.0, 0.0), axis=0, keepdims=True)
    for s in range(shares):
        delta_ref[:, s * cut : (s + 1) * cut] = tn(pick_ref[...], deltas[s]).astype(bf16)

    for k in range(1, peers):
        m_copy(other(k), other(k)).wait_recv()
    got = m_recv[:, :, :LANES].reshape(peers * block, LANES).astype(f32)
    chosen = (
        lax.rem(lax.broadcasted_iota(jnp.int32, (peers * block, wide), 0), block) // MOST
        == lax.broadcasted_iota(jnp.int32, (peers * block, wide), 1) // rank
    )

    def widened(a):
        return jnp.where(chosen, jnp.concatenate([a] * (wide // LANES), axis=1), 0.0).astype(bf16)

    grad_wide = widened(got)
    low_wide = widened(pltpu.roll(got, LANES // 2, 1))
    for c in range(0, part, 256):
        down_grad_ref[:, c : c + 256] = tn(
            grad_wide, x_recv[:, :, c : c + 256].reshape(peers * block, 256)
        )
    up_grad_ref[...] = adapter_scale * tn(low_wide, m_recv[:, :, LANES:].reshape(peers * block, cut))

    for j in range(1, owners):
        up_copy(lax.rem(d + j, owners), d).wait_send()
    for j in range(1, shares):
        s = lax.rem(f + j, shares)
        copy(up_all.at[f], up_all.at[f], vs.at[s], vr.at[f], d * shares + s).wait_send()
    for k in range(1, peers):
        x_copy(other(k), me).wait_send()
        low_copy(other(k), me).wait_send()
        m_copy(other(k), me).wait_send()


def adapters(pick, tokens, readout, adv, down, up, owners, shares, rank):
    buffer_rows, rows = pick.shape
    width, proj = tokens.shape[1], readout.shape[1]
    wide = up.shape[0]
    peers, block = owners * shares, buffer_rows // owners
    part, cut = width // shares, proj // shares
    dma = pltpu.SemaphoreType.DMA
    return pl.pallas_call(
        functools.partial(adapters_kernel, owners, shares, rank),
        out_shape=(
            jax.ShapeDtypeStruct((rows, proj), bf16),
            jax.ShapeDtypeStruct((1, rows), f32),
            jax.ShapeDtypeStruct((wide, part), f32),
            jax.ShapeDtypeStruct((wide, cut), f32),
        ),
        in_specs=[pl.BlockSpec(memory_space=pltpu.VMEM)] * 6,
        out_specs=tuple([pl.BlockSpec(memory_space=pltpu.VMEM)] * 4),
        scratch_shapes=[
            pltpu.VMEM((peers, block, part), bf16),
            pltpu.VMEM((peers, block, part), bf16),
            pltpu.VMEM((peers, block, LANES), f32),
            pltpu.VMEM((peers, block, LANES), f32),
            pltpu.VMEM((shares, owners, wide, cut), bf16),
            pltpu.VMEM((peers, block, LANES + cut), bf16),
            pltpu.VMEM((peers, block, LANES + cut), bf16),
            pltpu.VMEM((buffer_rows, proj), f32),
        ]
        + [dma((peers,))] * 6
        + [dma((owners,))] * 2
        + [dma((shares,))] * 2,
        compiler_params=pltpu.CompilerParams(
            collective_id=0, has_side_effects=True, vmem_limit_bytes=48 * 1024 * 1024
        ),
        cost_estimate=pl.CostEstimate(
            flops=8 * 10**9, bytes_accessed=12 * 2**20, transcendentals=buffer_rows
        ),
    )(pick, tokens, readout, adv, down, up)


def per_device(
    tokens,
    row_tenant_index,
    tenant_adapter_slot,
    live_row_counts,
    readout,
    advantage,
    base_value_matrix,
    adapter_down_maps,
    adapter_up_maps,
):
    rows, width = tokens.shape
    proj = base_value_matrix.shape[1]
    owners = lax.axis_size("dp")
    shares = lax.axis_size("fsdp")
    local, _, rank = adapter_down_maps.shape
    slots = tenant_adapter_slot.shape[0]
    per_owner = local * MOST
    buffer_rows = owners * per_owner
    peers = owners * shares
    part = width // shares
    proj_part = proj // shares
    both = ("dp", "fsdp")
    share = lax.axis_index("fsdp")

    base_all = lax.all_gather(base_value_matrix, "fsdp", axis=0, tiled=True)

    number = jnp.arange(rows, dtype=jnp.int32)
    live = number < live_row_counts[0]
    match = row_tenant_index == jnp.arange(slots, dtype=jnp.int32)[None, :]
    slot = jnp.sum(jnp.where(match, tenant_adapter_slot[None, :], 0), axis=1)
    same = (slot[:, None] == slot[None, :]) & live[None, :] & (number[None, :] < number[:, None])
    place = jnp.sum(same.astype(jnp.int32), axis=1)
    target = jnp.where(live, slot * MOST + place, buffer_rows)
    hit = jnp.arange(buffer_rows, dtype=jnp.int32)[:, None] == target[None, :]
    pick = hit.astype(bf16)

    if part % LANES == 0 and proj_part % LANES == 0 and LANES % (2 * rank) == 0:
        down = adapter_down_maps.transpose(0, 2, 1).reshape(local * rank, width)
        up = adapter_up_maps.reshape(local * rank, proj)
        delta, kl_rows, down_grad, up_grad = adapters(
            pick, tokens, readout, advantage.astype(f32)[None, :], down, up, owners, shares, rank
        )
        base = jnp.dot(tokens, base_all, preferred_element_type=f32)
        return (
            (base + delta.astype(f32)).astype(bf16),
            kl_rows[0],
            down_grad.reshape(local, rank, part).transpose(0, 2, 1),
            up_grad.reshape(local, rank, proj_part),
        )

    up_all = lax.all_gather(adapter_up_maps, "dp", axis=0, tiled=True)
    up_flat = up_all.reshape(slots * rank, proj)

    send_x = jnp.stack(
        [
            jnp.dot(pick, tokens[:, i * part : (i + 1) * part], preferred_element_type=f32)
            .astype(bf16)
            .reshape(owners, per_owner, part)
            for i in range(shares)
        ],
        axis=1,
    ).reshape(peers, per_owner, part)
    x = lax.all_to_all(send_x, both, split_axis=0, concat_axis=0, tiled=True)
    x = x.reshape(peers * per_owner, part)
    at = jnp.arange(peers * per_owner, dtype=jnp.int32) % per_owner // MOST
    chosen = at[:, None] == jnp.arange(local, dtype=jnp.int32)[None, :]

    down = lax.dynamic_slice_in_dim(adapter_down_maps, share * part, part, 1)
    every = jnp.einsum("au,wuq->awq", x, down, preferred_element_type=f32)
    low_part = jnp.sum(jnp.where(chosen[:, :, None], every, 0.0), axis=1)
    low_back = lax.all_to_all(
        low_part.reshape(peers, per_owner, rank), both, split_axis=0, concat_axis=0, tiled=True
    )
    low_buffer = jnp.sum(low_back.reshape(owners, shares, per_owner, rank), axis=1)
    low_buffer = rounded(low_buffer.reshape(buffer_rows, rank))

    low = jnp.einsum("br,bq->rq", pick, low_buffer, preferred_element_type=f32).astype(bf16)
    here = (slot[:, None] == jnp.arange(slots, dtype=jnp.int32)[None, :]) & live[:, None]
    wide = jnp.where(here[:, :, None], low[:, None, :], jnp.zeros((), bf16)).reshape(rows, slots * rank)
    delta = rounded(adapter_scale * jnp.dot(wide, up_flat, preferred_element_type=f32))
    delta32 = delta.astype(f32)

    dir32 = readout.astype(f32)
    gap = jnp.sum(delta32 * dir32, axis=1)
    kl_rows = jnp.where(live, jnp.exp(-gap) + gap - 1.0, 0.0)
    coeff = jnp.where(live, kl_weight * (1.0 - jnp.exp(-gap)) - advantage.astype(f32), 0.0)
    cot = rounded(coeff[:, None] * dir32)
    back = jnp.einsum("ni,ki->nk", cot, up_flat, preferred_element_type=f32)
    back = jnp.where(here[:, :, None], back.reshape(rows, slots, rank), 0.0)
    low_grad = rounded(adapter_scale * jnp.sum(back, axis=1))

    def sent(a):
        return jnp.dot(pick, a, preferred_element_type=f32).astype(bf16)

    small = jnp.concatenate([low_grad, low], axis=1)
    small = sent(small).reshape(owners, 1, per_owner, 2 * rank)
    large = sent(cot).reshape(owners, per_owner, shares, proj_part).transpose(0, 2, 1, 3)
    packed = jnp.concatenate(
        [jnp.broadcast_to(small, (owners, shares, per_owner, 2 * rank)), large], axis=3
    ).reshape(peers, per_owner, 2 * rank + proj_part)
    got = lax.all_to_all(packed, both, split_axis=0, concat_axis=0, tiled=True)
    got = got.reshape(peers * per_owner, 2 * rank + proj_part)

    none = jnp.zeros((), bf16)
    grad_wide = jnp.where(chosen[:, :, None], got[:, None, :rank], none)
    low_wide = jnp.where(chosen[:, :, None], got[:, None, rank : 2 * rank], none)
    down_map_gradient = jnp.einsum("md,mtr->tdr", x, grad_wide, preferred_element_type=f32)
    up_map_gradient = adapter_scale * jnp.einsum(
        "mtr,me->tre", low_wide, got[:, 2 * rank :], preferred_element_type=f32
    )
    base = jnp.dot(tokens, base_all, preferred_element_type=f32)
    values = (base + delta32).astype(bf16)
    return values, kl_rows, down_map_gradient, up_map_gradient


def solution(mesh):
    everywhere = ("groups", "dp", "fsdp")
    placed = (
        P(everywhere, None),
        P(everywhere, None),
        P(),
        P(everywhere),
        P(everywhere, None),
        P(everywhere),
        P("fsdp", None),
        P("dp", None, None),
        P("dp", None, None),
    )
    return jax.shard_map(
        per_device,
        mesh=mesh,
        in_specs=placed,
        out_specs=(
            P(everywhere, None),
            P(everywhere),
            P(("groups", "dp"), "fsdp", None),
            P(("groups", "dp"), None, "fsdp"),
        ),
        check_vma=False,
    )
```

time: 231 us -> 161 us (0.70)
  waiting for transfers between devices: 136 us -> 22.3 us
  Pallas kernels: 0 us -> 111 us
  local copies, waits for them, and re-layouts: 22.4 us -> 4.08 us
  blocking collectives: 17.4 us -> 0 us
  starting transfers between devices: 15.1 us -> 0.04 us
  matrix products: 19.9 us -> 8.45 us
  other arithmetic: 4.9 us -> 0.32 us
    pallas_call x0 -> x1, Pallas kernels: none -> 111 us  [adapters(): pl.pallas_call(functools.partial(adapters_kernel, owners, shares, rank),...]
    all_to_all x3 -> x0, waiting for transfers between devices: 73 us -> none  [the longest x1 59.1 us: per_device(): lax.all_to_all(send_x, 'dp', split_axis=0, concat_axis=0, tiled=True)]
    reduce_scatter x2 -> x0, waiting for transfers between devices: 62.7 us -> none  [the longest x1 54.7 us: per_device(): lax.psum_scatter(down_map_gradient, 'fsdp', scatter_dimension=1, tiled=True)]
    all_gather x1, waiting for transfers between devices: 0.02 us -> 21.6 us  [per_device(): base_all = lax.all_gather(base_value_matrix, 'fsdp', axis=0, tiled=True)]
    all_to_all x1 -> x0, blocking collectives: 17.4 us -> none  [per_device(): lax.all_to_all(send_cot, 'dp', split_axis=0, concat_axis=0, tiled=True)]
    all_to_all x3 -> x0, starting transfers between devices: 14.8 us -> none  [the longest x1 6.32 us: per_device(): lax.all_to_all(send_tag, 'dp', split_axis=0, concat_axis=0, tiled=True)]
    gather x4 -> x0, local copies, waits for them, and re-layouts: 14.6 us -> none  [the longest x1 8.69 us: per_device(): send_x = x_pad[source_row].reshape(owners, per_owner, width)]
    dot_general x5 -> x1, matrix products: 17.2 us -> 8.45 us  [per_device(): base = jnp.dot(tokens, base_all, preferred_element_type=f32)]
  transfers between devices with their start and end apart: 6 -> 1, of which waited for: 4 -> 1; matrix products, arithmetic and copies ran while one was open for 20% -> 0% of each run, Pallas kernels for 0% -> 69%
where the time goes in v1:
time: 161 us
  Pallas kernels  111 us (69%)
  waiting for transfers between devices  22.3 us (14%)
  between operations  14.8 us (9%)
  matrix products  8.45 us (5%)
  local copies, waits for them, and re-layouts  4.08 us (3%)
    pallas_call x1, Pallas kernels, adapters(): pl.pallas_call(functools.partial(adapters_kernel, owners, shares, rank),...  111 us
    all_gather x1, waiting for transfers between devices, per_device(): base_all = lax.all_gather(base_value_matrix, 'fsdp', axis=0, tiled=True)  21.6 us
    dot_general x1, matrix products, per_device(): base = jnp.dot(tokens, base_all, preferred_element_type=f32)  8.45 us
    unnamed x15, local copies, waits for them, and re-layouts  4.08 us
  transfers between devices with their start and end apart: 1, of which 1 were waited for; matrix products, arithmetic and copies ran while one was open for 0% of the time, Pallas kernels for 69%

profile of v1, /device:TPU:0, one launch (start us, length us, event | category | flops | bytes accessed | tf_op | source)
XLA Modules:
  0.0 161.1 jit_solution(842764434168492410)
XLA Ops:
  7.2 0.0 copy-start.5
  7.2 0.0 copy-start.4
  7.2 0.0 copy-start.3
  7.2 0.0 copy-start.2
  7.2 0.0 copy-start.1
  7.2 0.0 all-gather.2.cloned.1.call-start
  7.3 0.7 all-gather.2.cloned.1.call-update
  8.6 0.0 copy-done.5
  8.6 0.0 copy-done.4
  8.6 0.0 copy-done.3
  8.7 0.1 select_reduce_fusion
  8.7 0.2 convert_reduce_fusion
  9.0 0.0 copy-done.2
  9.0 0.0 copy-done.1
  9.0 0.0 copy-start
  9.0 1.7 %copy-done = bf16[256,5120]{1,0:T(8,128)(2,1)S(1)} copy-done((bf16[256,5120]{1,0:T(8,128)(2,1)S(1)}, bf16[256,5120]{1,0:T(8,128)(2,1)}, u32[]{:S(2)}) %copy-start) | copy-done | bytes 2621464
  10.7 111.1 %shard_map.120 = (bf16[256,1024]{1,0:T(8,128)(2,1)S(1)}, f32[1,256]{1,0:T(1,128)S(1)}, f32[256,1280]{1,0:T(8,128)S(1)}, f32[256,256]{1,0:T(8,128)S(1)}) custom-call(bf16[256,256]{1,0:T(8,128)(2,1)S(1)} %fusion.1.pick_ref, bf16[256,5120]{1,0:T(8,128)(2,1)S(1)} %copy-done, bf16[256,1024]{1,0:T(8,128)(2,1)S(1)} %copy-done.1, f32[1,256]{1,0:T(1,128)S(1)} %bitcast.20, ...), custom_call_target="tpu_custom_call" | custom-call | flops 8000000000 | bytes 12582912 | tf_op jit(solution)/shard_map/pallas_call | solution.py:221
  121.9 21.6 %all-gather.2.cloned.1.call-done = bf16[5120,1024]{1,0:T(8,128)(2,1)} async-done(((bf16[1280,1024]{1,0:T(8,128)(2,1)}), bf16[5120,1024]{1,0:T(8,128)(2,1)}) %all-gather.2.cloned.1.call-update) | async-done | bytes 10485776 | tf_op jit(solution)/shard_map/all_gather | solution.py:278
  143.5 8.4 %fusion = bf16[256,1024]{1,0:T(8,128)(2,1)} fusion(bf16[256,5120]{1,0:T(8,128)(2,1)} %tokens_ref.1, bf16[5120,1024]{1,0:T(8,128)(2,1)} %all-gather.2.cloned.1.call-done, bf16[256,1024]{1,0:T(8,128)(2,1)S(1)} %get-tuple-element.8), kind=kOutput, calls=%fused_computation.1 | convolution fusion | flops 2685140992 | bytes 14155776 | tf_op jit(solution)/shard_map/dot_general | solution.py:296
  152.0 0.6 copy.17
  152.5 1.1 copy.18
  153.6 0.7 copy.19
  (4 shorter events, 0.0 us)
Async XLA Ops:
  7.2 1.4 copy-start.5
  7.2 1.5 copy-start.4
  7.2 1.5 copy-start.3
  7.2 1.8 %copy-start.2 = (bf16[8,32,1024]{2,1,0:T(8,128)(2,1)S(1)}, bf16[8,32,1024]{2,1,0:T(8,128)(2,1)}, u32[]{:S(2)}) copy-start(bf16[8,32,1024]{2,1,0:T(8,128)(2,1)} %param.17) | copy-start | bytes 1572868
  7.2 1.8 %copy-start.1 = (bf16[256,1024]{1,0:T(8,128)(2,1)S(1)}, bf16[256,1024]{1,0:T(8,128)(2,1)}, u32[]{:S(2)}) copy-start(bf16[256,1024]{1,0:T(8,128)(2,1)} %readout_ref.1) | copy-start | bytes 1572868
  7.2 136.3 %all-gather.2.cloned.1.call-start = ((), (), s32[]{:S(2)}) async-start(), calls=%async_computation | async-start | bytes 13107200 | tf_op jit(solution)/shard_map/all_gather | solution.py:278
  9.0 1.7 %copy-start = (bf16[256,5120]{1,0:T(8,128)(2,1)S(1)}, bf16[256,5120]{1,0:T(8,128)(2,1)}, u32[]{:S(2)}) copy-start(bf16[256,5120]{1,0:T(8,128)(2,1)} %tokens_ref.1) | copy-start | bytes 7864324
Sparse Core Ops, SparseCore 0:
  9.6 133.8 all-gather.1

commit v2 on v1

--- a/solution.py
+++ b/solution.py
@@ -14,6 +14,8 @@
 bf16 = jnp.bfloat16
 f32 = jnp.float32
 LANES = 128
+PIECES = 2
+ORDER = (0, 1, 3, 2)
 
 
 def rounded(a):
@@ -30,14 +32,18 @@
 
 def adapters_kernel(
     owners, shares, rank,
-    pick_ref, tokens_ref, readout_ref, adv_ref, down_ref, up_ref,
-    delta_ref, kl_ref, down_grad_ref, up_grad_ref,
-    x_send, x_recv, low_send, low_recv, up_all, m_send, m_recv, dirs,
-    xs, xr, ls, lr, ms, mr, us, ur, vs, vr,
+    pick_ref, tokens_ref, readout_ref, adv_ref, down_ref, up_ref, base_ref,
+    values_ref, kl_ref, down_grad_ref, up_grad_ref,
+    x_send, x_recv, low_send, low_recv, up_all, m_send, m_recv, dirs, base_all, acc,
+    xs, xr, ls, lr, ms, mr, us, ur, vs, vr, bs, br,
 ):
     peers = owners * shares
     d, f = lax.axis_index("dp"), lax.axis_index("fsdp")
+    g = lax.axis_index("groups")
     me = d * shares + f
+    beside = f + 1 - 2 * lax.rem(f, 2)
+    across = lax.rem(f + 2, shares)
+    corner = lax.rem(beside + 2, shares)
     buffer_rows, rows = pick_ref.shape
     block = buffer_rows // owners
     wide = up_ref.shape[0]
@@ -70,7 +76,10 @@
         pl.semaphore_signal(
             barrier, inc=1, device_id=where_is(other(k)), device_id_type=pl.DeviceIdType.MESH
         )
-    pl.semaphore_wait(barrier, peers - 1)
+    pl.semaphore_signal(
+        barrier, inc=1, device_id={"groups": 1 - g}, device_id_type=pl.DeviceIdType.MESH
+    )
+    pl.semaphore_wait(barrier, peers)
 
     my_cut = pl.ds(pl.multiple_of(f * cut, LANES), cut)
 
@@ -94,14 +103,60 @@
             x_copy(o * shares + s, me).start()
     x_recv[me] = x_send[me]
 
-    def up_on(to_f, source):
-        return copy(up_all.at[f], up_all.at[source], vs.at[to_f], vr.at[source], d * shares + to_f)
+    half = base_ref.shape[0] // 2
+    piece = half // PIECES
+
+    def rows_of(h, c):
+        return pl.ds(pl.multiple_of(h * half + c * piece, 16), piece)
+
+    def base_copy(src, shard, h, c, sem, device):
+        return pltpu.make_async_remote_copy(
+            src_ref=src.at[rows_of(h, c)], dst_ref=base_all.at[shard, rows_of(h, c)],
+            send_sem=bs.at[sem], recv_sem=br.at[sem],
+            device_id=device, device_id_type=pl.DeviceIdType.MESH,
+        )
+
+    def over_x(shard, c):
+        return base_copy(base_ref, shard, g, c, c, {"fsdp": across})
+
+    def over_y(h, c):
+        return base_copy(base_all.at[across], across, h, c, PIECES + c, {"groups": 1 - g})
+
+    def over_core(shard, h, c, sem):
+        return base_copy(base_all.at[across], shard, h, c, sem, {"fsdp": beside})
+
+    def core_near(shard, c):
+        return over_core(shard, g, c, 2 * PIECES + c)
+
+    def core_far(shard, c):
+        return over_core(shard, 1 - g, c, 3 * PIECES + c)
+
+    def core_own(shard):
+        return pltpu.make_async_remote_copy(
+            src_ref=base_ref, dst_ref=base_all.at[shard],
+            send_sem=bs.at[4 * PIECES], recv_sem=br.at[4 * PIECES],
+            device_id={"fsdp": beside}, device_id_type=pl.DeviceIdType.MESH,
+        )
+
+    for c in range(PIECES):
+        over_x(f, c).start()
+    core_own(f).start()
+
+    def add_base(shard, ref, first=False):
+        columns = pl.ds(pl.multiple_of(shard * part, LANES), part)
+        for c in range(0, acc.shape[1], 512):
+            product = jnp.dot(
+                tokens_ref[:, columns], ref[:, c : c + 512], preferred_element_type=f32
+            )
+            acc[:, c : c + 512] = product if first else acc[:, c : c + 512] + product
+
+    def up_on(shard, sem, to):
+        return copy(up_all.at[shard], up_all.at[shard], vs.at[sem], vr.at[sem], d * shares + to)
 
     for j in range(1, owners):
         up_copy(d, lax.rem(d + j, owners)).wait_recv()
-    for j in range(1, shares):
-        s = lax.rem(f + j, shares)
-        copy(up_all.at[f], up_all.at[f], vs.at[s], vr.at[f], d * shares + s).start()
+    up_on(f, 0, across).start()
+    up_on(f, 1, beside).start()
 
     dirs[...] = jnp.dot(pick_ref[...], readout_ref[...], preferred_element_type=f32)
     hit = pick_ref[...].astype(f32) > 0.5
@@ -113,37 +168,58 @@
         == lax.broadcasted_iota(jnp.int32, (block, wide), 1) // rank
     )
 
+    fold = LANES // rank * MOST
+
     def low_of(q):
         every = jnp.where(own, nt(x_recv[q], down_ref[:, my_part]), 0.0)
         total = every[:, :LANES]
-        for g in range(1, wide // LANES):
-            total = total + every[:, g * LANES : (g + 1) * LANES]
-        return total
-
-    low_recv[me] = low_of(me)
-
-    def step(k, carry):
-        q = lax.rem(me + k, peers)
+        for n in range(1, wide // LANES):
+            total = total + every[:, n * LANES : (n + 1) * LANES]
+        return folded(total)
+
+    def folded(a):
+        a = a.reshape(a.shape[0] // fold, LANES // rank, MOST, LANES)
+        return jnp.sum(a, axis=1).reshape(a.shape[0] * MOST, LANES)
+
+    def unfolded(a):
+        a = a.reshape(a.shape[0] // MOST, 1, MOST, LANES)
+        a = jnp.concatenate([a] * (LANES // rank), axis=1)
+        return a.reshape(a.shape[0] * fold, LANES)
+
+    def low_step(q):
         x_copy(q, q).wait_recv()
         low_send[q] = low_of(q)
         low_copy(q, me).start()
-        return carry
-
-    lax.fori_loop(1, peers, step, 0)
-
-    for j in range(1, shares):
-        up_on(f, lax.rem(f + j, shares)).wait_recv()
+
+    low_recv[me] = low_of(me)
+    add_base(f, base_ref, first=True)
+    for n, j in enumerate(ORDER):
+        o = lax.rem(d + j, owners)
+        for i in range(shares):
+            if i or j:
+                low_step(o * shares + lax.rem(f + i, shares))
+        if n == 0:
+            up_on(across, 0, across).wait_recv()
+            up_on(across, 2, beside).start()
+        if n < PIECES:
+            over_x(across, n).wait_recv()
+            over_y(g, n).start()
+            core_near(across, n).start()
 
     for k in range(1, peers):
         low_copy(other(k), other(k)).wait_recv()
+    for c in range(PIECES):
+        over_y(1 - g, c).wait_recv()
+        core_far(across, c).start()
+    up_on(beside, 1, beside).wait_recv()
+    up_on(corner, 2, beside).wait_recv()
     blocks = []
     for o in range(owners):
         total = low_recv[o * shares]
         for s in range(1, shares):
             total = total + low_recv[o * shares + s]
-        blocks.append(total)
-    low = jnp.concatenate(blocks, axis=0).astype(bf16)
-    low32 = low.astype(f32)
+        blocks.append(unfolded(total))
+    low32 = jnp.concatenate(blocks, axis=0).astype(bf16).astype(f32)
     columns = owners * wide
     mine = (
         lax.broadcasted_iota(jnp.int32, (buffer_rows, columns), 0) // MOST
@@ -163,27 +239,42 @@
     for s in range(shares):
         cot = (coeff * dirs[:, s * cut : (s + 1) * cut]).astype(bf16)
         for o in range(owners):
-            m_send[o * shares + s, :, LANES:] = cot[o * block : (o + 1) * block]
+            m_send[o * shares + s, :block] = cot[o * block : (o + 1) * block]
         back = back + nt(cot, up_all[s].reshape(columns, cut))
     back = jnp.where(mine, back, 0.0)
     total = back[:, :LANES]
-    for g in range(1, columns // LANES):
-        total = total + back[:, g * LANES : (g + 1) * LANES]
-    packed = (adapter_scale * total + pltpu.roll(low32, LANES // 2, 1)).astype(bf16)
+    for n in range(1, columns // LANES):
+        total = total + back[:, n * LANES : (n + 1) * LANES]
+    kept = (
+        lax.rem(lax.broadcasted_iota(jnp.int32, (buffer_rows, LANES), 0) // MOST, LANES // rank)
+        == lax.broadcasted_iota(jnp.int32, (buffer_rows, LANES), 1) // rank
+    )
+    packed = jnp.concatenate(
+        [folded(adapter_scale * total), folded(jnp.where(kept, low32, 0.0))], axis=1
+    ).astype(bf16)
+    short = packed.shape[0] // owners
     for o in range(owners):
         for s in range(shares):
-            m_send[o * shares + s, :, :LANES] = packed[o * block : (o + 1) * block]
+            m_send[o * shares + s, block:] = packed[o * short : (o + 1) * short]
     for k in range(1, peers):
         m_copy(other(k), me).start()
     m_recv[me] = m_send[me]
 
     kl_ref[...] = jnp.sum(jnp.where(hit, small + gap - 1.0, 0.0), axis=0, keepdims=True)
+    core_own(beside).wait_recv()
+    add_base(beside, base_all.at[beside])
+    add_base(across, base_all.at[across])
+    for c in range(PIECES):
+        core_near(corner, c).wait_recv()
+        core_far(corner, c).wait_recv()
+    add_base(corner, base_all.at[corner])
     for s in range(shares):
-        delta_ref[:, s * cut : (s + 1) * cut] = tn(pick_ref[...], deltas[s]).astype(bf16)
+        at = slice(s * cut, (s + 1) * cut)
+        values_ref[:, at] = (acc[:, at] + tn(pick_ref[...], deltas[s])).astype(bf16)
 
     for k in range(1, peers):
         m_copy(other(k), other(k)).wait_recv()
-    got = m_recv[:, :, :LANES].reshape(peers * block, LANES).astype(f32)
+    got = m_recv[:, block:].astype(f32).reshape(peers * short, 2 * LANES)
     chosen = (
         lax.rem(lax.broadcasted_iota(jnp.int32, (peers * block, wide), 0), block) // MOST
         == lax.broadcasted_iota(jnp.int32, (peers * block, wide), 1) // rank
@@ -192,31 +283,38 @@
     def widened(a):
         return jnp.where(chosen, jnp.concatenate([a] * (wide // LANES), axis=1), 0.0).astype(bf16)
 
-    grad_wide = widened(got)
-    low_wide = widened(pltpu.roll(got, LANES // 2, 1))
+    grad_wide = widened(unfolded(got[:, :LANES]))
+    low_wide = widened(unfolded(got[:, LANES:]))
     for c in range(0, part, 256):
         down_grad_ref[:, c : c + 256] = tn(
             grad_wide, x_recv[:, :, c : c + 256].reshape(peers * block, 256)
         )
-    up_grad_ref[...] = adapter_scale * tn(low_wide, m_recv[:, :, LANES:].reshape(peers * block, cut))
+    up_grad_ref[...] = adapter_scale * tn(low_wide, m_recv[:, :block].reshape(peers * block, cut))
 
     for j in range(1, owners):
         up_copy(lax.rem(d + j, owners), d).wait_send()
-    for j in range(1, shares):
-        s = lax.rem(f + j, shares)
-        copy(up_all.at[f], up_all.at[f], vs.at[s], vr.at[f], d * shares + s).wait_send()
+    up_on(f, 0, across).wait_send()
+    up_on(f, 1, beside).wait_send()
+    up_on(across, 2, beside).wait_send()
+    for c in range(PIECES):
+        over_x(f, c).wait_send()
+        over_y(g, c).wait_send()
+        core_near(across, c).wait_send()
+        core_far(across, c).wait_send()
+    core_own(f).wait_send()
     for k in range(1, peers):
         x_copy(other(k), me).wait_send()
         low_copy(other(k), me).wait_send()
         m_copy(other(k), me).wait_send()
 
 
-def adapters(pick, tokens, readout, adv, down, up, owners, shares, rank):
+def adapters(pick, tokens, readout, adv, down, up, base, owners, shares, rank):
     buffer_rows, rows = pick.shape
     width, proj = tokens.shape[1], readout.shape[1]
     wide = up.shape[0]
     peers, block = owners * shares, buffer_rows // owners
     part, cut = width // shares, proj // shares
+    low_rows = block * rank // LANES
     dma = pltpu.SemaphoreType.DMA
     return pl.pallas_call(
         functools.partial(adapters_kernel, owners, shares, rank),
@@ -226,28 +324,31 @@
             jax.ShapeDtypeStruct((wide, part), f32),
             jax.ShapeDtypeStruct((wide, cut), f32),
         ),
-        in_specs=[pl.BlockSpec(memory_space=pltpu.VMEM)] * 6,
+        in_specs=[pl.BlockSpec(memory_space=pltpu.VMEM)] * 7,
         out_specs=tuple([pl.BlockSpec(memory_space=pltpu.VMEM)] * 4),
         scratch_shapes=[
             pltpu.VMEM((peers, block, part), bf16),
             pltpu.VMEM((peers, block, part), bf16),
-            pltpu.VMEM((peers, block, LANES), f32),
-            pltpu.VMEM((peers, block, LANES), f32),
+            pltpu.VMEM((peers, low_rows, LANES), f32),
+            pltpu.VMEM((peers, low_rows, LANES), f32),
             pltpu.VMEM((shares, owners, wide, cut), bf16),
-            pltpu.VMEM((peers, block, LANES + cut), bf16),
-            pltpu.VMEM((peers, block, LANES + cut), bf16),
+            pltpu.VMEM((peers, block + low_rows, cut), bf16),
+            pltpu.VMEM((peers, block + low_rows, cut), bf16),
             pltpu.VMEM((buffer_rows, proj), f32),
+            pltpu.VMEM((shares, part, proj), bf16),
+            pltpu.VMEM((rows, proj), f32),
         ]
         + [dma((peers,))] * 6
         + [dma((owners,))] * 2
-        + [dma((shares,))] * 2,
+        + [dma((shares,))] * 2
+        + [dma((4 * PIECES + 1,))] * 2,
         compiler_params=pltpu.CompilerParams(
-            collective_id=0, has_side_effects=True, vmem_limit_bytes=48 * 1024 * 1024
+            collective_id=0, has_side_effects=True, vmem_limit_bytes=56 * 1024 * 1024
         ),
         cost_estimate=pl.CostEstimate(
             flops=8 * 10**9, bytes_accessed=12 * 2**20, transcendentals=buffer_rows
         ),
-    )(pick, tokens, readout, adv, down, up)
+    )(pick, tokens, readout, adv, down, up, base)
 
 
 def per_device(
@@ -275,8 +376,6 @@
     both = ("dp", "fsdp")
     share = lax.axis_index("fsdp")
 
-    base_all = lax.all_gather(base_value_matrix, "fsdp", axis=0, tiled=True)
-
     number = jnp.arange(rows, dtype=jnp.int32)
     live = number < live_row_counts[0]
     match = row_tenant_index == jnp.arange(slots, dtype=jnp.int32)[None, :]
@@ -287,20 +386,30 @@
     hit = jnp.arange(buffer_rows, dtype=jnp.int32)[:, None] == target[None, :]
     pick = hit.astype(bf16)
 
-    if part % LANES == 0 and proj_part % LANES == 0 and LANES % (2 * rank) == 0:
+    fits = (
+        lax.axis_size("groups") == 2
+        and owners == len(ORDER)
+        and shares == 4
+        and part % 256 == 0
+        and proj_part == 2 * LANES
+        and LANES % rank == 0
+        and local * rank % LANES == 0
+    )
+    if fits:
         down = adapter_down_maps.transpose(0, 2, 1).reshape(local * rank, width)
         up = adapter_up_maps.reshape(local * rank, proj)
-        delta, kl_rows, down_grad, up_grad = adapters(
-            pick, tokens, readout, advantage.astype(f32)[None, :], down, up, owners, shares, rank
-        )
-        base = jnp.dot(tokens, base_all, preferred_element_type=f32)
+        values, kl_rows, down_grad, up_grad = adapters(
+            pick, tokens, readout, advantage.astype(f32)[None, :], down, up, base_value_matrix,
+            owners, shares, rank,
+        )
         return (
-            (base + delta.astype(f32)).astype(bf16),
+            values,
             kl_rows[0],
             down_grad.reshape(local, rank, part).transpose(0, 2, 1),
             up_grad.reshape(local, rank, proj_part),
         )
 
+    base_all = lax.all_gather(base_value_matrix, "fsdp", axis=0, tiled=True)
     up_all = lax.all_gather(adapter_up_maps, "dp", axis=0, tiled=True)
     up_flat = up_all.reshape(slots * rank, proj)
 

time: 161 us -> 135 us (0.84); the launches traced: 161 us -> 133 us
  waiting for transfers between devices: 22.3 us -> 0 us
  between operations: 14.8 us -> 1.31 us
  Pallas kernels: 111 us -> 122 us
  matrix products: 8.45 us -> 0 us
  other arithmetic: 0.32 us -> 2.89 us
  local copies, waits for them, and re-layouts: 4.08 us -> 6.33 us
    all_gather x1 -> x0, waiting for transfers between devices: 21.6 us -> none  [per_device(): base_all = lax.all_gather(base_value_matrix, 'fsdp', axis=0, tiled=True)]
    pallas_call x1, Pallas kernels: 111 us -> 122 us  [adapters(): pl.pallas_call(functools.partial(adapters_kernel, owners, shares, rank),...]
    dot_general x1 -> x0, matrix products: 8.45 us -> none  [per_device(): base = jnp.dot(tokens, base_all, preferred_element_type=f32)]
    unnamed x15 -> x6, local copies, waits for them, and re-layouts: 4.08 us -> 6.33 us
  transfers between devices with their start and end apart: 1 -> 0, of which waited for: 1 -> 0; matrix products, arithmetic and copies ran while one was open for 0% -> 0% of each run, Pallas kernels for 69% -> 0%
where the time goes in v2:
time: 135 us; the launch traced here: 133 us
  Pallas kernels  122 us (90%)
  local copies, waits for them, and re-layouts  6.33 us (5%)
  other arithmetic  2.89 us (2%)
    pallas_call x1, Pallas kernels, adapters(): pl.pallas_call(functools.partial(adapters_kernel, owners, shares, rank),...  122 us
    unnamed x6, local copies, waits for them, and re-layouts  6.33 us

profile of v2, /device:TPU:0, one launch (start us, length us, event | category | flops | bytes accessed | tf_op | source)
XLA Modules:
  0.0 132.9 jit_solution(9081280886607201009)
XLA Ops:
  1.3 0.8 select_reduce_fusion
  2.1 0.2 convert_reduce_fusion
  2.3 1.2 broadcast_in_dim.35
  3.5 0.7 fusion.pick_ref
  4.2 122.4 %shard_map.120 = (bf16[256,1024]{1,0:T(8,128)(2,1)}, f32[1,256]{1,0:T(1,128)}, f32[256,1280]{1,0:T(8,128)}, f32[256,256]{1,0:T(8,128)}) custom-call(bf16[256,256]{1,0:T(8,128)(2,1)} %fusion.pick_ref, bf16[256,5120]{1,0:T(8,128)(2,1)} %tokens_ref.1, bf16[256,1024]{1,0:T(8,128)(2,1)} %readout_ref.1, f32[1,256]{1,0:T(1,128)} %bitcast.20, ...), custom_call_target="tpu_custom_call" | custom-call | flops 8000000000 | bytes 12582912 | tf_op jit(solution)/shard_map/pallas_call | solution.py:319
  126.5 0.0 copy-start
  126.6 1.9 %copy.18 = bf16[256,1024]{1,0:T(8,128)(2,1)} copy(bf16[256,1024]{1,0:T(8,128)(2,1)} %get-tuple-element.16) | data formatting | bytes 1048576
  128.5 1.2 copy.19
  129.7 2.5 %copy.20 = f32[8,1280,32]{1,2,0:T(8,128)} copy(f32[8,1280,32]{1,2,0:T(8,128)} %bitcast.14) | data formatting | bytes 2621440
  132.2 0.0 copy-done
  132.2 0.7 copy.21
  (2 shorter events, 0.0 us)
Async XLA Ops:
  126.5 5.6 %copy-start = (f32[256,256]{1,0:T(8,128)S(1)}, f32[256,256]{1,0:T(8,128)}, u32[]{:S(2)}) copy-start(f32[256,256]{1,0:T(8,128)} %get-tuple-element.11) | copy-start | bytes 786436

commit v3 on v2

--- a/solution.py
+++ b/solution.py
@@ -35,7 +35,7 @@
     pick_ref, tokens_ref, readout_ref, adv_ref, down_ref, up_ref, base_ref,
     values_ref, kl_ref, down_grad_ref, up_grad_ref,
     x_send, x_recv, low_send, low_recv, up_all, m_send, m_recv, dirs, base_all, acc,
-    xs, xr, ls, lr, ms, mr, us, ur, vs, vr, bs, br,
+    xs, xr, ls, lr, ms, mr, us, ur, ws, wr, vs, vr, bs, br,
 ):
     peers = owners * shares
     d, f = lax.axis_index("dp"), lax.axis_index("fsdp")
@@ -83,8 +83,21 @@
 
     my_cut = pl.ds(pl.multiple_of(f * cut, LANES), cut)
 
+    def up_rows(h):
+        return pl.ds(pl.multiple_of(h * (wide // 2), 16), wide // 2)
+
     def up_copy(to_d, source):
-        return copy(up_ref.at[:, my_cut], up_all.at[f, source], us.at[to_d], ur.at[source], to_d * shares + f)
+        return copy(
+            up_ref.at[up_rows(g), my_cut], up_all.at[f, source, up_rows(g)],
+            us.at[to_d], ur.at[source], to_d * shares + f,
+        )
+
+    def up_over_y(o, h):
+        return pltpu.make_async_remote_copy(
+            src_ref=up_all.at[f, o, up_rows(h)], dst_ref=up_all.at[f, o, up_rows(h)],
+            send_sem=ws.at[o], recv_sem=wr.at[o],
+            device_id={"groups": 1 - g}, device_id_type=pl.DeviceIdType.MESH,
+        )
 
     for j in range(1, owners):
         up_copy(lax.rem(d + j, owners), d).start()
@@ -138,8 +151,6 @@
             device_id={"fsdp": beside}, device_id_type=pl.DeviceIdType.MESH,
         )
 
-    for c in range(PIECES):
-        over_x(f, c).start()
     core_own(f).start()
 
     def add_base(shard, ref, first=False):
@@ -155,6 +166,9 @@
 
     for j in range(1, owners):
         up_copy(d, lax.rem(d + j, owners)).wait_recv()
+        up_over_y(lax.rem(d + j, owners), g).start()
+    for j in range(1, owners):
+        up_over_y(lax.rem(d + j, owners), 1 - g).wait_recv()
     up_on(f, 0, across).start()
     up_on(f, 1, beside).start()
 
@@ -164,18 +178,23 @@
 
     my_part = pl.ds(pl.multiple_of(f * part, LANES), part)
     own = (
-        lax.broadcasted_iota(jnp.int32, (block, wide), 0) // MOST
-        == lax.broadcasted_iota(jnp.int32, (block, wide), 1) // rank
+        lax.rem(lax.broadcasted_iota(jnp.int32, (shares * block, wide), 0), block) // MOST
+        == lax.broadcasted_iota(jnp.int32, (shares * block, wide), 1) // rank
     )
 
     fold = LANES // rank * MOST
 
-    def low_of(q):
-        every = jnp.where(own, nt(x_recv[q], down_ref[:, my_part]), 0.0)
+    def low_of(o):
+        sources = x_recv[pl.ds(o * shares, shares)].reshape(shares * block, part)
+        every = nt(sources, down_ref[:, my_part])
+        every = jnp.where(own, every, 0.0)
         total = every[:, :LANES]
         for n in range(1, wide // LANES):
             total = total + every[:, n * LANES : (n + 1) * LANES]
-        return folded(total)
+        total = folded(total)
+        each = total.shape[0] // shares
+        for i in range(shares):
+            low_send[o * shares + i] = total[i * each : (i + 1) * each]
 
     def folded(a):
         a = a.reshape(a.shape[0] // fold, LANES // rank, MOST, LANES)
@@ -186,25 +205,28 @@
         a = jnp.concatenate([a] * (LANES // rank), axis=1)
         return a.reshape(a.shape[0] * fold, LANES)
 
-    def low_step(q):
-        x_copy(q, q).wait_recv()
-        low_send[q] = low_of(q)
-        low_copy(q, me).start()
-
-    low_recv[me] = low_of(me)
     add_base(f, base_ref, first=True)
     for n, j in enumerate(ORDER):
         o = lax.rem(d + j, owners)
-        for i in range(shares):
-            if i or j:
-                low_step(o * shares + lax.rem(f + i, shares))
+        turns = range(0 if j else 1, shares)
+        for i in turns:
+            q = o * shares + lax.rem(f + i, shares)
+            x_copy(q, q).wait_recv()
+        low_of(o)
+        for i in turns:
+            low_copy(o * shares + lax.rem(f + i, shares), me).start()
+        if n == 0:
+            low_recv[me] = low_send[me]
         if n == 0:
             up_on(across, 0, across).wait_recv()
             up_on(across, 2, beside).start()
-        if n < PIECES:
-            over_x(across, n).wait_recv()
-            over_y(g, n).start()
-            core_near(across, n).start()
+            for c in range(PIECES):
+                over_x(f, c).start()
+        if n >= 4 - PIECES:
+            c = n - 4 + PIECES
+            over_x(across, c).wait_recv()
+            over_y(g, c).start()
+            core_near(across, c).start()
 
     for k in range(1, peers):
         low_copy(other(k), other(k)).wait_recv()
@@ -293,6 +315,7 @@
 
     for j in range(1, owners):
         up_copy(lax.rem(d + j, owners), d).wait_send()
+        up_over_y(lax.rem(d + j, owners), g).wait_send()
     up_on(f, 0, across).wait_send()
     up_on(f, 1, beside).wait_send()
     up_on(across, 2, beside).wait_send()
@@ -339,7 +362,7 @@
             pltpu.VMEM((rows, proj), f32),
         ]
         + [dma((peers,))] * 6
-        + [dma((owners,))] * 2
+        + [dma((owners,))] * 4
         + [dma((shares,))] * 2
         + [dma((4 * PIECES + 1,))] * 2,
         compiler_params=pltpu.CompilerParams(

time: 135 us -> 129 us (0.956)
  Pallas kernels: 122 us -> 116 us
    pallas_call x1, Pallas kernels: 122 us -> 116 us  [adapters(): pl.pallas_call(functools.partial(adapters_kernel, owners, shares, rank),...]
where the time goes in v3:
time: 129 us; the launch traced here: 127 us
  Pallas kernels  116 us (90%)
  local copies, waits for them, and re-layouts  6.33 us (5%)
  other arithmetic  2.89 us (2%)
  between operations  1.31 us (1%)
    pallas_call x1, Pallas kernels, adapters(): pl.pallas_call(functools.partial(adapters_kernel, owners, shares, rank),...  116 us
    unnamed x6, local copies, waits for them, and re-layouts  6.33 us

profile of v3, /device:TPU:0, one launch (start us, length us, event | category | flops | bytes accessed | tf_op | source)
XLA Modules:
  0.0 127.0 jit_solution(1501830317305059630)
XLA Ops:
  1.3 0.8 select_reduce_fusion
  2.1 0.2 convert_reduce_fusion
  2.3 1.2 broadcast_in_dim.35
  3.5 0.7 fusion.pick_ref
  4.2 116.4 %shard_map.120 = (bf16[256,1024]{1,0:T(8,128)(2,1)}, f32[1,256]{1,0:T(1,128)}, f32[256,1280]{1,0:T(8,128)}, f32[256,256]{1,0:T(8,128)}) custom-call(bf16[256,256]{1,0:T(8,128)(2,1)} %fusion.pick_ref, bf16[256,5120]{1,0:T(8,128)(2,1)} %tokens_ref.1, bf16[256,1024]{1,0:T(8,128)(2,1)} %readout_ref.1, f32[1,256]{1,0:T(1,128)} %bitcast.20, ...), custom_call_target="tpu_custom_call" | custom-call | flops 8000000000 | bytes 12582912 | tf_op jit(solution)/shard_map/pallas_call | solution.py:342
  120.6 0.0 copy-start
  120.6 1.9 %copy.18 = bf16[256,1024]{1,0:T(8,128)(2,1)} copy(bf16[256,1024]{1,0:T(8,128)(2,1)} %get-tuple-element.16) | data formatting | bytes 1048576
  122.6 1.2 copy.19
  123.8 2.5 %copy.20 = f32[8,1280,32]{1,2,0:T(8,128)} copy(f32[8,1280,32]{1,2,0:T(8,128)} %bitcast.14) | data formatting | bytes 2621440
  126.3 0.0 copy-done
  126.3 0.7 copy.21
  (2 shorter events, 0.0 us)
Async XLA Ops:
  120.6 5.6 %copy-start = (f32[256,256]{1,0:T(8,128)S(1)}, f32[256,256]{1,0:T(8,128)}, u32[]{:S(2)}) copy-start(f32[256,256]{1,0:T(8,128)} %get-tuple-element.11) | copy-start | bytes 786436
